TPU v7x, 512 devices: a whole 4x4x16 slice. The times are simulated.
512 devices in a mesh: row: 32 (over z, x_lo), col: 16 (over y, x_hi, core).
Axes of the slice: x: 4 (x_hi: 2, x_lo: 2; x = x_hi * 2 + x_lo), y: 4, z: 16, core: 2. Of those that a mesh axis runs over, the one named last changes fastest.
Arguments:
- x_window: bfloat16 [3, 2048, 512], P(None, 'row', 'col'), may hold values from -6 to 6
- y_window: float32 [3, 2048], P(None, 'row'), may hold values from -6 to 6
- block_order: int32 [3], replicated, may hold values from 0 to 2, each once
- diag_inverse: bfloat16 [3, 2048, 2048], P(None, 'row'), may hold values from -0.5 to 1.5, as said below
- panel_window: bfloat16 [3, 2048, 2048], P(None, 'row', 'col'), may hold values from -0.078125 to 0.078125
- panel_trail: bfloat16 [4096, 3, 2048], P('row', None, 'col'), may hold values from -0.078125 to 0.078125
- x_trail: bfloat16 [4096, 512], P('row', 'col'), may hold values from -6 to 6
- y_trail: float32 [4096], P('row'), may hold values from -6 to 6
Outputs:
- whitened: bfloat16 [3, 2048, 512], P(None, 'row', 'col')
- white_resp: bfloat16 [3, 2048], P(None, 'row')
- trail_rhs: float32 [4096, 512], P('row', 'col')
- trail_resp: float32 [4096], P('row')
- normal_part: float32 [512, 512], P('row')
- right_part: float32 [512], P('row')
Inputs may be any that keep to these rules, and one draw needn't show every extreme that they name: Each diag_inverse[s] is lower triangular with a positive diagonal.
All inputs are finite; a program needn't handle non-finite values.
Results may differ from a plain program's by a relative error of at most 0.014.
Values may be sent and summed in bfloat16 or wider, within the bound.
A program may use at most 64 MiB of HBM per device.

v0:
```python
import jax
import jax.numpy as jnp
from jax import lax
from jax.sharding import PartitionSpec as P


def shards(
    x_window, y_window, block_order, diag_inverse, panel_window, panel_trail, x_trail, y_trail
):
    steps = x_window.shape[0]
    own_rows = x_window.shape[1]
    own_cols = x_window.shape[2]
    width = panel_window.shape[2]
    block_rows = own_rows * lax.axis_size("row")
    full_cols = own_cols * lax.axis_size("col")
    normal_rows = full_cols // lax.axis_size("row")
    col_start = lax.axis_index("col") * width
    normal_start = lax.axis_index("row") * normal_rows
    trail_rows = x_trail.shape[0]
    solved_cols = []
    solved_resp = []
    out_tiles = []
    out_resp = []
    trail_total = jnp.zeros((trail_rows, full_cols), jnp.float32)
    trail_resp_total = jnp.zeros((trail_rows,), jnp.float32)
    gram = jnp.zeros((normal_rows, full_cols), jnp.float32)
    right = jnp.zeros((normal_rows,), jnp.float32)
    for s in range(steps):
        stored = block_order[s]
        pending = lax.dynamic_index_in_dim(x_window, stored, 0, keepdims=False).astype(jnp.float32)
        pending_resp = lax.dynamic_index_in_dim(y_window, stored, 0, keepdims=False)
        if s > 0:
            first = s * (s - 1) // 2
            factors = panel_window[first : first + s]
            earlier = jnp.stack(solved_cols)
            earlier_resp = jnp.stack(solved_resp)
            update = jnp.einsum("trw,twp->rp", factors, earlier, preferred_element_type=jnp.float32)
            update_resp = jnp.einsum(
                "trw,tw->r", factors, earlier_resp, preferred_element_type=jnp.float32
            )
            pending = pending - lax.psum_scatter(update, "col", scatter_dimension=1, tiled=True)
            pending_resp = pending_resp - lax.psum(update_resp, "col")
        residual = pending.astype(jnp.bfloat16)
        resid_resp = pending_resp.astype(jnp.bfloat16)
        whole, whole_resp = (
            lax.all_gather(residual, "row", axis=0, tiled=True),
            lax.all_gather(resid_resp, "row", axis=0, tiled=True),
        )
        inverse = diag_inverse[s]
        tile = jnp.dot(inverse, whole, preferred_element_type=jnp.float32).astype(jnp.bfloat16)
        tile_resp = jnp.dot(inverse, whole_resp, preferred_element_type=jnp.float32).astype(
            jnp.bfloat16
        )
        out_tiles.append(tile)
        out_resp.append(tile_resp)
        all_rows, all_resp = (
            lax.all_gather(tile, "row", axis=0, tiled=True),
            lax.all_gather(tile_resp, "row", axis=0, tiled=True),
        )
        mine = lax.all_to_all(all_rows, "col", split_axis=0, concat_axis=1, tiled=True)
        mine_resp = lax.dynamic_slice_in_dim(all_resp, col_start, width, 0)
        solved_cols.append(mine)
        solved_resp.append(mine_resp)
        factor_rows = panel_trail[:, s, :]
        trail_total = trail_total + jnp.dot(factor_rows, mine, preferred_element_type=jnp.float32)
        trail_resp_total = trail_resp_total + jnp.dot(
            factor_rows, mine_resp, preferred_element_type=jnp.float32
        )
        slab = lax.dynamic_slice_in_dim(mine, normal_start, normal_rows, 1)
        gram = gram + lax.dot_general(
            slab, mine, (((0,), (0,)), ((), ())), preferred_element_type=jnp.float32
        )
        right = right + lax.dot_general(
            slab, mine_resp, (((0,), (0,)), ((), ())), preferred_element_type=jnp.float32
        )
    summed = lax.psum(trail_total.astype(jnp.bfloat16), "col").astype(jnp.float32)
    share = lax.dynamic_slice_in_dim(summed, lax.axis_index("col") * own_cols, own_cols, 1)
    trail_rhs = x_trail.astype(jnp.float32) - share
    gram, right, resp_sum = lax.psum((gram, right, trail_resp_total), "col")
    trail_resp = y_trail - resp_sum
    scale = 1.0 / (steps * block_rows)
    whitened = jnp.stack(out_tiles)
    white_resp = jnp.stack(out_resp)
    return (whitened, white_resp, trail_rhs, trail_resp, gram * scale, right * scale)


def solution(mesh):
    in_specs = (
        P(None, "row", "col"),
        P(None, "row"),
        P(),
        P(None, "row", None),
        P(None, "row", "col"),
        P("row", None, "col"),
        P("row", "col"),
        P("row"),
    )
    out_specs = (
        P(None, "row", "col"),
        P(None, "row"),
        P("row", "col"),
        P("row"),
        P("row", None),
        P("row"),
    )
    return jax.shard_map(shards, mesh=mesh, in_specs=in_specs, out_specs=out_specs, check_vma=False)
```

profile of v0, /device:TPU:1, one launch (start us, length us, event | category | flops | bytes accessed | tf_op | source)
XLA Modules:
  0.0 1263.4 jit_solution(17524989272356092082)
XLA Ops:
  7.2 1.4 fusion.84
  14.5 61.7 %all-gather = bf16[1,2048,32]{2,0,1:T(2,128)(2,1)S(1)} all-gather(bf16[1,64,32]{2,0,1:T(2,128)(2,1)S(1)} %copy.62), channel_id=2, replica_groups=mesh['row'=32,'col'=16] {'row'}, dimensions={1}, use_global_device_ids=true | all-gather | bytes 135168 | tf_op jit(solution)/shard_map/all_gather | solution.py:46
  76.2 0.5 copy.42
  76.8 0.6 copy-done
  77.4 0.2 fusion.2
  77.5 46.4 %all-gather.2 = bf16[32,64,32]{1,2,0:T(8,128)(2,1)S(1)} all-gather(bf16[1,64,32]{1,2,0:T(8,128)(2,1)S(1)} %fusion.2), channel_id=1, replica_groups=mesh['row'=32,'col'=16] {'row'}, dimensions={0}, use_global_device_ids=true | all-gather | bytes 135168 | tf_op jit(solution)/shard_map/all_gather | solution.py:57
  124.2 0.7 copy.45
  124.9 34.9 %all-to-all-start = ((bf16[16,128,32]{1,2,0:T(8,128)(2,1)}), bf16[16,128,32]{1,2,0:T(8,128)(2,1)S(1)}, u32[]{:S(2)}, u32[]{:S(2)}) async-start(bf16[16,128,32]{1,2,0:T(8,128)(2,1)} %copy.45), calls=%async_computation | async-start | bytes 262144 | tf_op jit(solution)/shard_map/all_to_all | solution.py:60
  159.9 0.6 copy-done.5
  160.5 1.3 dynamic-slice
  162.4 0.2 dynamic-update-slice
  162.7 47.3 %all-reduce = bf16[2048]{0:T(1024)(128)(2,1)S(1)} all-reduce(bf16[2048]{0:T(1024)(128)(2,1)S(1)} %dynamic-update-slice), channel_id=3, replica_groups=mesh['row'=32,'col'=16] {'row'}, use_global_device_ids=true, to_apply=%add | all-reduce | flops 2048 | bytes 8192 | tf_op jit(solution)/shard_map/all_gather | solution.py:47
  210.2 0.2 dynamic-update-slice.1
  210.4 46.7 %all-reduce.1 = bf16[2048]{0:T(1024)(128)(2,1)S(1)} all-reduce(bf16[2048]{0:T(1024)(128)(2,1)S(1)} %dynamic-update-slice.1), channel_id=1, replica_groups=mesh['row'=32,'col'=16] {'row'}, use_global_device_ids=true, to_apply=%add.1 | all-reduce | flops 2048 | bytes 8192
  257.2 0.2 convolution_bitcast_fusion.9
  257.4 60.9 %psum.42 = f32[64]{0:T(128)S(1)} all-reduce(f32[64]{0:T(128)S(1)} %convolution_bitcast_fusion.9), channel_id=1, replica_groups=mesh['row'=32,'col'=16] {'col'}, use_global_device_ids=true, to_apply=%region_2.3 | all-reduce | flops 64 | bytes 512 | tf_op jit(solution)/shard_map/psum | solution.py:42
  318.3 0.2 dynamic-update-slice.2
  318.5 47.1 %all-reduce.2 = bf16[2048]{0:T(1024)(128)(2,1)S(1)} all-reduce(bf16[2048]{0:T(1024)(128)(2,1)S(1)} %dynamic-update-slice.2), channel_id=1, replica_groups=mesh['row'=32,'col'=16] {'row'}, use_global_device_ids=true, to_apply=%add.2 | all-reduce | flops 2048 | bytes 8192
  365.8 0.2 dynamic-update-slice.3
  366.0 47.2 %all-reduce.3 = bf16[2048]{0:T(1024)(128)(2,1)S(1)} all-reduce(bf16[2048]{0:T(1024)(128)(2,1)S(1)} %dynamic-update-slice.3), channel_id=1, replica_groups=mesh['row'=32,'col'=16] {'row'}, use_global_device_ids=true, to_apply=%add.3 | all-reduce | flops 2048 | bytes 8192
  413.4 60.5 %psum.43 = f32[64]{0:T(128)S(1)} all-reduce(f32[64]{0:T(128)S(1)} %convolution_bitcast_fusion.2), channel_id=1, replica_groups=mesh['row'=32,'col'=16] {'col'}, use_global_device_ids=true, to_apply=%region_3.4 | all-reduce | flops 64 | bytes 512 | tf_op jit(solution)/shard_map/psum | solution.py:42
  473.9 0.2 dynamic-update-slice.4
  474.2 47.3 %all-reduce.4 = bf16[2048]{0:T(1024)(128)(2,1)S(1)} all-reduce(bf16[2048]{0:T(1024)(128)(2,1)S(1)} %dynamic-update-slice.4), channel_id=1, replica_groups=mesh['row'=32,'col'=16] {'row'}, use_global_device_ids=true, to_apply=%add.4 | all-reduce | flops 2048 | bytes 8192
  521.6 0.2 fusion.9
  521.7 0.2 dynamic-update-slice.5
  521.9 46.9 %all-reduce.5 = bf16[2048]{0:T(1024)(128)(2,1)S(1)} all-reduce(bf16[2048]{0:T(1024)(128)(2,1)S(1)} %dynamic-update-slice.5), channel_id=1, replica_groups=mesh['row'=32,'col'=16] {'row'}, use_global_device_ids=true, to_apply=%add.5 | all-reduce | flops 2048 | bytes 8192
  568.9 0.2 convolution_bitcast_fusion.8
  569.0 0.2 fusion.8
  569.2 0.2 fusion.7
  569.6 0.6 pad_maximum_fusion.1
  570.4 0.2 convolution_bitcast_fusion.5
  570.6 0.8 copy.58
  571.6 0.2 fusion.35
  571.7 105.4 %reduce-scatter.7.cloned.1.call-done = f32[32,64]{1,0:T(8,128)} async-done(((f32[512,64]{1,0:T(8,128)}), f32[32,64]{1,0:T(8,128)}) %reduce-scatter.7.cloned.1.call-update) | async-done | bytes 8208
  677.1 0.8 copy.59
  678.0 50.2 %all-gather.3 = bf16[32,64,32]{1,2,0:T(8,128)(2,1)S(1)} all-gather(bf16[1,64,32]{1,2,0:T(8,128)(2,1)S(1)} %copy.46), channel_id=1, replica_groups=mesh['row'=32,'col'=16] {'row'}, dimensions={0}, use_global_device_ids=true | all-gather | bytes 135168 | tf_op jit(solution)/shard_map/all_gather | solution.py:46
  728.3 0.3 reshape.65
  728.6 0.2 fusion.3
  728.7 46.4 %all-gather.4 = bf16[32,64,32]{1,2,0:T(8,128)(2,1)S(1)} all-gather(bf16[1,64,32]{1,2,0:T(8,128)(2,1)S(1)} %fusion.3), channel_id=1, replica_groups=mesh['row'=32,'col'=16] {'row'}, dimensions={0}, use_global_device_ids=true | all-gather | bytes 135168 | tf_op jit(solution)/shard_map/all_gather | solution.py:57
  775.4 0.7 copy.50
  776.1 34.8 %all-to-all-start.1 = ((bf16[16,128,32]{1,2,0:T(8,128)(2,1)}), bf16[16,128,32]{1,2,0:T(8,128)(2,1)S(1)}, u32[]{:S(2)}, u32[]{:S(2)}) async-start(bf16[16,128,32]{1,2,0:T(8,128)(2,1)} %copy.50), calls=%async_computation.1 | async-start | bytes 262144 | tf_op jit(solution)/shard_map/all_to_all | solution.py:60
  811.0 7.5 all-to-all-done.1
  818.8 0.8 copy.60
  819.6 0.2 convolution_add_fusion.1
  820.0 81.2 %reduce-scatter.9.cloned.1.call-done = f32[32,64]{1,0:T(8,128)} async-done(((f32[512,64]{1,0:T(8,128)}), f32[32,64]{1,0:T(8,128)}) %reduce-scatter.9.cloned.1.call-update) | async-done | bytes 8208
  901.2 0.8 copy.61
  902.1 50.2 %all-gather.5 = bf16[32,64,32]{1,2,0:T(8,128)(2,1)S(1)} all-gather(bf16[1,64,32]{1,2,0:T(8,128)(2,1)S(1)} %copy.53), channel_id=1, replica_groups=mesh['row'=32,'col'=16] {'row'}, dimensions={0}, use_global_device_ids=true | all-gather | bytes 135168 | tf_op jit(solution)/shard_map/all_gather | solution.py:46
  952.3 0.3 reshape.69
  952.6 0.2 fusion.4
  952.8 46.4 %all-gather.6 = bf16[32,64,32]{1,2,0:T(8,128)(2,1)S(1)} all-gather(bf16[1,64,32]{1,2,0:T(8,128)(2,1)S(1)} %fusion.4), channel_id=1, replica_groups=mesh['row'=32,'col'=16] {'row'}, dimensions={0}, use_global_device_ids=true | all-gather | bytes 135168 | tf_op jit(solution)/shard_map/all_gather | solution.py:57
  999.5 0.7 copy.56
  1000.1 34.8 %all-to-all-start.2 = ((bf16[16,128,32]{1,2,0:T(8,128)(2,1)}), bf16[16,128,32]{1,2,0:T(8,128)(2,1)S(1)}, u32[]{:S(2)}, u32[]{:S(2)}) async-start(bf16[16,128,32]{1,2,0:T(8,128)(2,1)} %copy.56), calls=%async_computation.2 | async-start | bytes 262144 | tf_op jit(solution)/shard_map/all_to_all | solution.py:60
  1035.0 0.2 fusion.6
  1035.1 0.6 pad_maximum_fusion
  1035.8 6.8 all-to-all-done.2
  1042.6 0.2 fusion.5
  1042.9 60.2 %all-reduce.6 = (f32[128]{0:T(128)S(1)}, f32[16,512]{1,0:T(8,128)S(1)}, f32[16]{0:T(128)S(1)}) all-reduce(f32[128]{0:T(128)S(1)} %fusion.7, f32[16,512]{1,0:T(8,128)S(1)} %convolution_add_fusion.2, f32[16]{0:T(128)S(1)} %fusion.5), channel_id=1, replica_groups=mesh['row'=32,'col'=16] {'col'}, use_global_device_ids=true, to_apply=%region_5.6 | all-reduce | flops 8336 | bytes 66688 | tf_op jit(solution)/shard_map/psum | solution.py:79
  1103.1 0.6 broadcast_multiply_fusion
  1103.7 0.8 fusion.1
  1104.6 0.6 copy-done.6
  1105.3 0.5 sub.23
  1105.8 0.5 broadcast_multiply_fusion.1
  1106.3 149.3 %all-reduce.9.cloned.1.call-done = bf16[128,512]{0,1:T(8,128)(2,1)} async-done(((bf16[128,512]{0,1:T(8,128)(2,1)}), bf16[128,512]{0,1:T(8,128)(2,1)}) %all-reduce.9.cloned.1.call-update) | async-done | bytes 131088 | tf_op jit(solution)/shard_map/psum | solution.py:76
  1255.6 1.3 convert_subtract_fusion.2
  (59 shorter events, 3.3 us)
Async XLA Ops:
  7.2 7.2 copy-start.3
  76.2 1.1 copy-start
  124.9 445.3 %all-to-all-start = ((bf16[16,128,32]{1,2,0:T(8,128)(2,1)}), bf16[16,128,32]{1,2,0:T(8,128)(2,1)S(1)}, u32[]{:S(2)}, u32[]{:S(2)}) async-start(bf16[16,128,32]{1,2,0:T(8,128)(2,1)} %copy.45), calls=%async_computation | async-start | bytes 262144 | tf_op jit(solution)/shard_map/all_to_all | solution.py:60
  159.8 0.7 copy-start.5
  159.8 517.3 %reduce-scatter.7.cloned.1.call-start = ((), (), s32[]{:S(2)}) async-start(), calls=%async_computation.6 | async-start | bytes 278528
  210.0 47.2 %copy-start.2 = (bf16[3,64,128]{2,1,0:T(8,128)(2,1)S(1)}, bf16[3,64,128]{2,1,0:T(8,128)(2,1)}, u32[]{:S(2)}) copy-start(bf16[3,64,128]{2,1,0:T(8,128)(2,1)} %param.12) | copy-start | bytes 147460
  521.6 47.3 %copy-start.1 = (bf16[128,3,128]{2,0,1:T(8,128)(2,1)S(1)}, bf16[128,3,128]{2,0,1:T(8,128)(2,1)}, u32[]{:S(2)}) copy-start(bf16[128,3,128]{2,0,1:T(8,128)(2,1)} %param.13) | copy-start | bytes 294916
  776.1 42.4 %all-to-all-start.1 = ((bf16[16,128,32]{1,2,0:T(8,128)(2,1)}), bf16[16,128,32]{1,2,0:T(8,128)(2,1)S(1)}, u32[]{:S(2)}, u32[]{:S(2)}) async-start(bf16[16,128,32]{1,2,0:T(8,128)(2,1)} %copy.50), calls=%async_computation.1 | async-start | bytes 262144 | tf_op jit(solution)/shard_map/all_to_all | solution.py:60
  810.8 90.3 %reduce-scatter.9.cloned.1.call-start = ((), (), s32[]{:S(2)}) async-start(), calls=%async_computation.7 | async-start | bytes 278528
  1000.1 42.4 %all-to-all-start.2 = ((bf16[16,128,32]{1,2,0:T(8,128)(2,1)}), bf16[16,128,32]{1,2,0:T(8,128)(2,1)S(1)}, u32[]{:S(2)}, u32[]{:S(2)}) async-start(bf16[16,128,32]{1,2,0:T(8,128)(2,1)} %copy.56), calls=%async_computation.2 | async-start | bytes 262144 | tf_op jit(solution)/shard_map/all_to_all | solution.py:60
  1034.9 220.7 %all-reduce.9.cloned.1.call-start = ((), (), s32[]{:S(2)}) async-start(), calls=%async_computation.5 | async-start | bytes 262144 | tf_op jit(solution)/shard_map/psum | solution.py:76
  1104.6 151.0 %copy-start.4 = (bf16[128,32]{0,1:T(8,128)(2,1)S(1)}, bf16[128,32]{0,1:T(8,128)(2,1)}, u32[]{:S(2)}) copy-start(bf16[128,32]{0,1:T(8,128)(2,1)} %param.14) | copy-start | bytes 24580
  1104.6 0.7 copy-start.6
Sparse Core Ops, SparseCore 0:
  571.6 105.5 reduce-scatter.6
  819.8 81.3 reduce-scatter.8
  1104.7 150.7 all-reduce.8
where the time goes:
time: 1260 us
  blocking collectives  765 us (61%)
  waiting for transfers between devices  350 us (28%)
  starting transfers between devices  105 us (8%)
  between operations  20.4 us (2%)
  local copies, waits for them, and re-layouts  14.1 us (1%)
    unnamed x5, blocking collectives  235 us
    unnamed x5, waiting for transfers between devices  187 us
    all_gather x3, blocking collectives, shards(): lax.all_gather(residual, 'row', axis=0, tiled=True)  162 us
    psum x1, waiting for transfers between devices, shards(): lax.psum(trail_total.astype(jnp.bfloat16), 'col').astype(jnp.float32)  149 us
    all_gather x3, blocking collectives, shards(): lax.all_gather(tile, 'row', axis=0, tiled=True)  139 us
    psum x2, blocking collectives, shards(): pending_resp = pending_resp - lax.psum(update_resp, 'col')  121 us
    all_to_all x3, starting transfers between devices, shards(): lax.all_to_all(all_rows, 'col', split_axis=0, concat_axis=1, tiled=True)  104 us
    psum x1, blocking collectives, shards(): gram, right, resp_sum = lax.psum((gram, right, trail_resp_total), 'col')  60.2 us
  transfers between devices with their start and end apart: 6, of which 5 were waited for; matrix products, arithmetic and copies ran while one was open for 1% of the time, Pallas kernels for 0%

commit v1 on v0

v1 whole, which is shorter than its diff:
```python
import jax
import jax.numpy as jnp
from jax import lax
from jax.experimental import pallas as pl
from jax.experimental.pallas import tpu as pltpu
from jax.sharding import PartitionSpec as P

MESH = pl.DeviceIdType.MESH
F32 = jnp.float32
BF16 = jnp.bfloat16


def dot_t(a, b):
    return lax.dot_general(a, b, (((1,), (1,)), ((), ())), preferred_element_type=F32)


def twice(a):
    return jnp.concatenate([a, a], axis=0)


def kernel(
    order,
    x_ref,
    y_ref,
    d_hbm,
    l_ref,
    t_ref,
    white_out,
    trail_out,
    normal_out,
    right_out,
    ubuf,
    fbuf,
    xt,
    dv,
    lv,
    tsrc,
    tv,
    ah,
    nb,
    ybuf,
    d_sem,
    us_sem,
    ur_sem,
    fs_sem,
    fr_sem,
    ls_sem,
    lr_sem,
    ts_sem,
    tr_sem,
    as_sem,
    ar_sem,
    ns_sem,
    nr_sem,
):
    row = lax.axis_index("row")
    col = lax.axis_index("col")
    z = row // 2
    xl = row % 2
    n_row, n_col = 32, 16

    def row_peer(k):
        half = k // 2
        return lax.rem(row + n_row // 2 + jnp.where(k % 2 == 0, half, n_row - half - 1), n_row)

    def col_peer(k):
        return lax.rem(col + 1 + k, n_col)

    load_d = pltpu.make_async_copy(d_hbm, dv, d_sem)
    load_d.start()
    barrier = pltpu.get_barrier_semaphore()

    def greet_row(k, carry):
        pl.semaphore_signal(barrier, inc=1, device_id={"row": row_peer(k)}, device_id_type=MESH)
        return carry

    def greet_col(k, carry):
        pl.semaphore_signal(barrier, inc=1, device_id={"col": col_peer(k)}, device_id_type=MESH)
        return carry

    lax.fori_loop(0, n_row - 1, greet_row, 0)
    lax.fori_loop(0, n_col - 1, greet_col, 0)

    lane = lax.broadcasted_iota(jnp.int32, (16, 128), 1)
    low = lane < 64
    mine = jnp.where(xl == 0, lane, 127 - lane) < 64
    lane1 = lax.broadcasted_iota(jnp.int32, (1, 128), 1)
    mine1 = jnp.where(xl == 0, lane1, 127 - lane1) < 64
    eye = (
        lax.broadcasted_iota(jnp.int32, (48, 32), 0) == lax.broadcasted_iota(jnp.int32, (48, 32), 1)
    ).astype(F32).astype(BF16)
    sub = lax.broadcasted_iota(jnp.int32, (48, 128), 0)

    ybuf[...] = jnp.zeros_like(ybuf)

    def stored(s):
        block = x_ref[order[s]]
        ybuf[s, 0:1, 0:64] = y_ref[order[s]]
        y = ybuf[s]
        y = y + pltpu.roll(y, 64, 1)
        return dot_t(eye, twice(block)) + jnp.where(sub >= 32, y[0:1, :], 0.0)

    def send(p, value):
        ubuf[p, row] = jnp.where(mine, value[0:16], value[16:32]).astype(BF16)
        fbuf[p, row] = jnp.where(mine1, value[32:33], 0.0)

        def push(k, carry):
            peer = {"row": row_peer(k)}
            pltpu.make_async_remote_copy(
                ubuf.at[p, row], ubuf.at[p, row], us_sem.at[p], ur_sem.at[p], peer, MESH
            ).start()
            pltpu.make_async_remote_copy(
                fbuf.at[p, row], fbuf.at[p, row], fs_sem.at[p], fr_sem.at[p], peer, MESH
            ).start()
            return carry

        lax.fori_loop(0, n_row - 1, push, 0)

    def await_bytes(ref, sem):
        pltpu.make_async_copy(ref, ref, sem).wait()

    def receive(p, slot):
        await_bytes(ubuf.at[p, 0 : n_row - 1], ur_sem.at[p])
        await_bytes(fbuf.at[p, 0 : n_row - 1], fr_sem.at[p])

        def unpack(k, carry):
            even = ubuf[p, 2 * k].astype(F32)
            odd = ubuf[p, 2 * k + 1].astype(F32)
            at = pl.ds(pl.multiple_of(128 * k, 128), 128)
            xt[slot, 0:16, at] = jnp.where(low, even, odd).astype(BF16)
            xt[slot, 16:32, at] = pltpu.roll(jnp.where(low, odd, even), 64, 1).astype(BF16)
            resp = fbuf[p, 2 * k] + fbuf[p, 2 * k + 1]
            xt[slot, 32:48, at] = jnp.broadcast_to(resp, (16, 128)).astype(BF16)
            return carry

        lax.fori_loop(0, n_row // 2, unpack, 0, unroll=4)

    def rounded(value):
        return value.astype(BF16).astype(F32)

    my_cols = pl.ds(pl.multiple_of(128 * col, 128), 128)

    def send_l():
        def push(k, carry):
            pltpu.make_async_remote_copy(
                l_ref, lv.at[:, :, my_cols], ls_sem, lr_sem, {"col": col_peer(k)}, MESH
            ).start()
            return carry

        lax.fori_loop(0, n_col - 1, push, 0)
        lv[:, :, my_cols] = l_ref[...]

    def send_t(s):
        def push(k, carry):
            pltpu.make_async_remote_copy(
                tsrc.at[s],
                tv.at[s, :, my_cols],
                ts_sem.at[s],
                tr_sem.at[s],
                {"col": col_peer(k)},
                MESH,
            ).start()
            return carry

        lax.fori_loop(0, n_col - 1, push, 0)
        tv[s, :, my_cols] = tsrc[s]

    half = pl.ds(pl.multiple_of(16 * xl, 16), 16)

    def send_a(s):
        @pl.when(col == z)
        def _():
            ah[s] = xt[s, half, :]

            def push(k, carry):
                pltpu.make_async_remote_copy(
                    ah.at[s], ah.at[s], as_sem.at[s], ar_sem.at[s], {"col": col_peer(k)}, MESH
                ).start()
                return carry

            lax.fori_loop(0, n_col - 1, push, 0)

    def receive_a(s):
        @pl.when(col != z)
        def _():
            await_bytes(ah.at[s], ar_sem.at[s])

    def trail_term(s):
        await_bytes(tv.at[s, :, 0 : 128 * (n_col - 1)], tr_sem.at[s])
        return dot_t(xt[s], tv[s])

    def gram_term(s):
        receive_a(s)
        left = ah[s]
        own = xt[s, 0:32, :]
        return dot_t(left, twice(twice(own))), dot_t(left, xt[s, 32:48, :])

    pending0 = stored(0)
    pending1 = stored(1)
    pending2 = stored(2)
    for s in range(3):
        tsrc[s] = t_ref[s]

    pl.semaphore_wait(barrier, n_row - 1 + n_col - 1)

    send(0, pending0)
    send_l()
    load_d.wait()
    receive(0, 3)
    white0 = rounded(dot_t(xt[3], twice(dv[0])))
    send(1, white0)
    white_out[0] = white0
    send_t(0)

    receive(1, 0)
    await_bytes(lv.at[:, :, 0 : 128 * (n_col - 1)], lr_sem)
    send(2, pending1 - dot_t(xt[0], twice(lv[0])))
    send_a(0)
    send_t(1)
    pending2 = pending2 - dot_t(xt[0], twice(lv[1]))

    receive(2, 3)
    white1 = rounded(dot_t(xt[3], twice(dv[1])))
    send(3, white1)
    white_out[1] = white1
    send_t(2)
    trail = trail_term(0)

    receive(3, 1)
    send(4, pending2 - dot_t(xt[1], twice(lv[2])))
    send_a(1)
    trail = trail + trail_term(1)
    gram, right = gram_term(0)

    receive(4, 3)
    white2 = rounded(dot_t(xt[3], twice(dv[2])))
    send(5, white2)
    white_out[2] = white2
    gram1, right1 = gram_term(1)

    receive(5, 2)
    send_a(2)
    trail_out[...] = trail + trail_term(2)
    gram2, right2 = gram_term(2)
    scale = 1.0 / 6144
    right_out[...] = (right + right1 + right2) * scale
    gram = (gram + gram1 + gram2) * scale
    nb[col] = jnp.where(lane // 32 == col % 4, gram, 0.0)

    def push_n(k, carry):
        pltpu.make_async_remote_copy(
            nb.at[col], nb.at[col], ns_sem, nr_sem, {"col": col_peer(k)}, MESH
        ).start()
        return carry

    lax.fori_loop(0, n_col - 1, push_n, 0)
    for p in range(6):
        await_bytes(ubuf.at[p, 0 : n_row - 1], us_sem.at[p])
        await_bytes(fbuf.at[p, 0 : n_row - 1], fs_sem.at[p])
    await_bytes(lv.at[:, :, 0 : 128 * (n_col - 1)], ls_sem)
    for s in range(3):
        await_bytes(tv.at[s, :, 0 : 128 * (n_col - 1)], ts_sem.at[s])

        @pl.when(col == z)
        def _():
            def drain(k, carry):
                await_bytes(ah.at[s], as_sem.at[s])
                return carry

            lax.fori_loop(0, n_col - 1, drain, 0)

    await_bytes(nb.at[0 : n_col - 1], ns_sem)
    await_bytes(nb.at[0 : n_col - 1], nr_sem)
    for j in range(4):
        normal_out[:, 128 * j : 128 * j + 128] = (
            nb[4 * j] + nb[4 * j + 1] + nb[4 * j + 2] + nb[4 * j + 3]
        )


def shards(
    x_window, y_window, block_order, diag_inverse, panel_window, panel_trail, x_trail, y_trail
):
    vmem = pl.BlockSpec(memory_space=pltpu.VMEM)
    dma = pltpu.SemaphoreType.DMA
    white, trail, normal, right = pl.pallas_call(
        kernel,
        name="substitution",
        out_shape=(
            jax.ShapeDtypeStruct((3, 48, 128), F32),
            jax.ShapeDtypeStruct((48, 128), F32),
            jax.ShapeDtypeStruct((16, 512), F32),
            jax.ShapeDtypeStruct((16, 16), F32),
        ),
        in_specs=[
            pl.BlockSpec(memory_space=pltpu.SMEM),
            vmem,
            vmem,
            pl.BlockSpec(memory_space=pl.ANY),
            vmem,
            vmem,
        ],
        out_specs=(vmem, vmem, vmem, vmem),
        scratch_shapes=[
            pltpu.VMEM((6, 32, 16, 128), BF16),
            pltpu.VMEM((6, 32, 1, 128), F32),
            pltpu.VMEM((4, 48, 2048), BF16),
            pltpu.VMEM((3, 64, 2048), BF16),
            pltpu.VMEM((3, 64, 2048), BF16),
            pltpu.VMEM((3, 128, 128), BF16),
            pltpu.VMEM((3, 128, 2048), BF16),
            pltpu.VMEM((3, 16, 2048), BF16),
            pltpu.VMEM((16, 16, 128), F32),
            pltpu.VMEM((3, 8, 128), F32),
            dma,
            dma((6,)),
            dma((6,)),
            dma((6,)),
            dma((6,)),
            dma,
            dma,
            dma((3,)),
            dma((3,)),
            dma((3,)),
            dma((3,)),
            dma,
            dma,
        ],
        compiler_params=pltpu.CompilerParams(
            collective_id=0, has_side_effects=True, vmem_limit_bytes=48 * 1024 * 1024
        ),
    )(
        block_order,
        x_window,
        y_window[:, None, :],
        diag_inverse,
        panel_window,
        panel_trail.transpose(1, 0, 2),
    )
    whitened = white[:, 0:32, 0:64].transpose(0, 2, 1).astype(BF16)
    white_resp = white[:, 32, 0:64].astype(BF16)
    trail_rhs = x_trail.astype(F32) - trail[0:32].T
    trail_resp = y_trail - trail[32]
    return whitened, white_resp, trail_rhs, trail_resp, normal, right[:, 0]


def solution(mesh):
    in_specs = (
        P(None, "row", "col"),
        P(None, "row"),
        P(),
        P(None, "row", None),
        P(None, "row", "col"),
        P("row", None, "col"),
        P("row", "col"),
        P("row"),
    )
    out_specs = (
        P(None, "row", "col"),
        P(None, "row"),
        P("row", "col"),
        P("row"),
        P("row", None),
        P("row"),
    )
    return jax.shard_map(shards, mesh=mesh, in_specs=in_specs, out_specs=out_specs, check_vma=False)
```

time: 1260 us -> 99 us (0.08)
  blocking collectives: 765 us -> 0 us
  waiting for transfers between devices: 350 us -> 0 us
  starting transfers between devices: 105 us -> 0 us
  Pallas kernels: 0 us -> 90.8 us
  between operations: 20.4 us -> 0.7 us
    all_gather x7 -> x0, blocking collectives: 349 us -> none  [the longest x3 162 us: shards(): lax.all_gather(residual, 'row', axis=0, tiled=True)]
    unnamed x5 -> x0, blocking collectives: 235 us -> none
    unnamed x5 -> x0, waiting for transfers between devices: 187 us -> none
    psum x3 -> x0, blocking collectives: 182 us -> none  [the longest x2 121 us: shards(): pending_resp = pending_resp - lax.psum(update_resp, 'col')]
    psum x1 -> x0, waiting for transfers between devices: 149 us -> none  [shards(): lax.psum(trail_total.astype(jnp.bfloat16), 'col').astype(jnp.float32)]
    all_to_all x3 -> x0, starting transfers between devices: 104 us -> none  [shards(): lax.all_to_all(all_rows, 'col', split_axis=0, concat_axis=1, tiled=True)]
    pallas_call x0 -> x1, Pallas kernels: none -> 90.8 us  [shards(): pl.pallas_call(kernel, name='substitution', out_shape=(jax.ShapeDtypeStru...]
    all_to_all x3 -> x0, waiting for transfers between devices: 14.3 us -> none  [shards(): lax.all_to_all(all_rows, 'col', split_axis=0, concat_axis=1, tiled=True)]
  transfers between devices with their start and end apart: 6 -> 0, of which waited for: 5 -> 0; matrix products, arithmetic and copies ran while one was open for 1% -> 0% of each run, Pallas kernels for 0% -> 0%
where the time goes in v1:
time: 99 us; the launch traced here: 98.6 us
  Pallas kernels  90.8 us (92%)
  local copies, waits for them, and re-layouts  6.01 us (6%)
  other arithmetic  1.13 us (1%)
    pallas_call x1, Pallas kernels, shards(): pl.pallas_call(kernel, name='substitution', out_shape=(jax.ShapeDtypeStru...  90.8 us
    unnamed x15, local copies, waits for them, and re-layouts  4.07 us

profile of v1, /device:TPU:1, one launch (start us, length us, event | category | flops | bytes accessed | tf_op | source)
XLA Modules:
  0.0 98.6 jit_solution(5743934883549635623)
XLA Ops:
  0.6 0.0 copy-start.2
  0.6 0.7 broadcast_in_dim.3.y_ref
  1.3 0.0 copy-start.3
  1.3 0.8 copy.15.x_ref
  2.2 0.0 copy-done.2
  2.2 0.0 copy-done.3
  2.2 0.0 copy-start
  2.2 1.1 %copy-done = bf16[3,64,2048]{2,1,0:T(8,128)(2,1)S(1)} copy-done((bf16[3,64,2048]{2,1,0:T(8,128)(2,1)S(1)}, bf16[3,64,2048]{2,1,0:T(8,128)(2,1)}, u32[]{:S(2)}) %copy-start) | copy-done | bytes 786456
  3.3 0.0 copy-start.1
  3.3 0.9 copy-done.1
  4.2 90.8 %substitution.1 = (f32[3,48,128]{2,1,0:T(8,128)S(1)}, f32[48,128]{1,0:T(8,128)S(1)}, f32[16,512]{1,0:T(8,128)S(1)}, f32[16,16]{1,0:T(8,128)S(1)}) custom-call(s32[3]{0:T(128)S(1)} %copy-done.3, bf16[3,64,32]{2,1,0:T(8,128)(2,1)S(1)} %copy.15.x_ref, f32[3,1,64]{2,1,0:T(1,128)S(1)} %broadcast_in_dim.3.y_ref, bf16[3,64,2048]{2,1,0:T(8,128)(2,1)S(1)} %copy-done, ...), custom_call_target="tpu_custom_call" | custom-call | tf_op jit(solution)/shard_map/substitution/pallas_call | solution.py:285
  95.1 0.0 copy-start.5
  95.1 0.0 copy-start.4
  95.1 0.6 slice_reduce_fusion
  95.7 0.0 copy-done.5
  95.7 0.5 bitcast_subtract_fusion.1
  96.2 0.0 copy-done.4
  96.2 0.6 bitcast_subtract_fusion
  96.9 0.6 slice_bitcast_fusion
  97.5 0.6 copy.18
  98.0 0.6 copy.20
  (2 shorter events, 0.0 us)
Async XLA Ops:
  0.6 1.6 %copy-start.2 = (bf16[3,64,128]{2,1,0:T(8,128)(2,1)S(1)}, bf16[3,64,128]{2,1,0:T(8,128)(2,1)}, u32[]{:S(2)}) copy-start(bf16[3,64,128]{2,1,0:T(8,128)(2,1)} %l_ref.1) | copy-start | bytes 147460
  1.3 0.9 copy-start.3
  2.2 1.1 %copy-start = (bf16[3,64,2048]{2,1,0:T(8,128)(2,1)S(1)}, bf16[3,64,2048]{2,1,0:T(8,128)(2,1)}, u32[]{:S(2)}) copy-start(bf16[3,64,2048]{2,1,0:T(8,128)(2,1)} %d_hbm.1) | copy-start | bytes 2359300
  3.3 0.9 copy-start.1
  95.1 0.7 copy-start.5
  95.1 1.2 %copy-start.4 = (bf16[128,32]{0,1:T(8,128)(2,1)S(1)}, bf16[128,32]{0,1:T(8,128)(2,1)}, u32[]{:S(2)}) copy-start(bf16[128,32]{0,1:T(8,128)(2,1)} %param.14) | copy-start | bytes 24580

commit v2 on v0

v2 whole, which is shorter than its diff:
```python
import jax
import jax.numpy as jnp
from jax import lax
from jax.experimental import pallas as pl
from jax.experimental.pallas import tpu as pltpu
from jax.sharding import PartitionSpec as P

MESH = pl.DeviceIdType.MESH
F32 = jnp.float32
BF16 = jnp.bfloat16
NZ = 16
NC = 16
X1, W0, R2, W1, W2 = range(5)
WHITE = (W0, W1, W2)


def dot_t(a, b):
    return lax.dot_general(a, b, (((1,), (1,)), ((), ())), preferred_element_type=F32)


def dot_n(a, b):
    return lax.dot_general(a, b, (((1,), (0,)), ((), ())), preferred_element_type=F32)


def rounded(value):
    return value.astype(BF16).astype(F32)


def await_bytes(ref, sem):
    pltpu.make_async_copy(ref, ref, sem).wait()


def repeat(count, body):
    def step(k, carry):
        body(k)
        return carry

    lax.fori_loop(0, count, step, 0)


def kernel(
    order,
    x_ref,
    y_ref,
    d_ref,
    l_ref,
    t_ref,
    white_out,
    trail_out,
    normal_out,
    right_out,
    xsrc,
    ysrc,
    xbuf,
    ybuf,
    xr,
    ltsrc,
    ltex,
    lg,
    mv,
    gx,
    gy,
    hx,
    dv,
    lv,
    tv,
    ah,
    nb,
    tmp,
    own_sem,
    xs_sem,
    xr_sem,
    ys_sem,
    yr_sem,
    es_sem,
    er_sem,
    ds_sem,
    dr_sem,
    ls_sem,
    lr_sem,
    gs_sem,
    gr_sem,
    zs_sem,
    zr_sem,
    ms_sem,
    mr_sem,
    qs_sem,
    qr_sem,
    hs_sem,
    hr_sem,
    ts_sem,
    tr_sem,
    as_sem,
    ar_sem,
    ns_sem,
    nr_sem,
):
    row = lax.axis_index("row")
    c = lax.axis_index("col")
    z = row // 2
    x = row % 2
    spot = x * NC + c
    beside = {"row": 2 * z + 1 - x, "col": c}

    def far(k):
        half = (k + 1) // 2
        return lax.rem(z + NZ // 2 + jnp.where(k % 2 == 1, half, NZ - half), NZ)

    def along(k):
        return {"row": 2 * far(k) + x, "col": c}

    def across(k):
        return {"row": 2 * far(k) + 1 - x, "col": c}

    def turn(k):
        return {"row": row, "col": lax.rem(c + 1 + k, NC)}

    def over(k):
        return {"row": 2 * z + 1 - x, "col": lax.rem(c + k, NC)}

    def plane(k):
        other = lax.rem(spot + 1 + k, 2 * NC)
        return {"row": 2 * z + other // NC, "col": other % NC}

    def push(src, dst, send_sem, recv_sem, peer):
        pltpu.make_async_remote_copy(src, dst, send_sem, recv_sem, peer, MESH).start()

    at_c = pl.ds(pl.multiple_of(128 * c, 128), 128)
    at_z = pl.ds(pl.multiple_of(128 * z, 128), 128)
    own_half = pl.ds(pl.multiple_of(64 * x, 64), 64)
    other_half = pl.ds(pl.multiple_of(64 - 64 * x, 64), 64)

    barrier = pltpu.get_barrier_semaphore()

    def greet(peer):
        pl.semaphore_signal(barrier, inc=1, device_id=peer, device_id_type=MESH)

    repeat(NZ - 1, lambda k: greet(along(k)))
    repeat(NZ - 1, lambda k: greet(across(k)))
    repeat(2 * NC - 1, lambda k: greet(plane(k)))

    pltpu.make_async_copy(d_ref, dv.at[:, own_half, :], own_sem.at[0]).start()
    pltpu.make_async_copy(l_ref.at[1], lv.at[own_half, at_c], lr_sem).start()

    lane = lax.broadcasted_iota(jnp.int32, (16, 128), 1)
    first = x == 0
    mine = jnp.where(first, lane, 127 - lane) < 64
    mine1 = mine[0:1]

    tmp[...] = jnp.zeros_like(tmp)
    for s in range(3):
        tmp[0:32, 0:64] = x_ref[order[s]].astype(F32)
        tmp[32:33, 0:64] = y_ref[pl.ds(order[s], 1), :]
        both = tmp[...]
        both = jnp.where(first, both, pltpu.roll(both, 64, 1))
        xsrc[s, 0] = jnp.where(first, both[0:16], both[16:32]).astype(BF16)
        xsrc[s, 1] = jnp.where(first, both[16:32], both[0:16]).astype(BF16)
        ysrc[s] = both[32:33]
    eye = (
        lax.broadcasted_iota(jnp.int32, (128, 128), 0)
        == lax.broadcasted_iota(jnp.int32, (128, 128), 1)
    ).astype(F32).astype(BF16)
    lane_l = lax.broadcasted_iota(jnp.int32, (128, 128), 1)
    mine_l = jnp.where(first, lane_l, 127 - lane_l) < 64
    for q in range(2):
        block = l_ref[2 * q]
        turned = dot_t(eye, jnp.concatenate([block, block], axis=0))
        ltsrc[q] = jnp.where(mine_l, turned, 0.0).astype(BF16)

        def clear(k):
            @pl.when(k > z)
            def _():
                lg[q, :, pl.ds(pl.multiple_of(128 * k, 128), 128)] = jnp.zeros((64, 128), BF16)

        repeat(NZ, clear)

    xbuf[2, row] = xsrc[0, 0]
    ybuf[2, row] = ysrc[0]

    pl.semaphore_wait(barrier, 2 * (NZ - 1) + 2 * NC - 1)

    def push_x0(k):
        push(xsrc.at[0, 0], xbuf.at[2, row], xs_sem, xr_sem, along(k))
        push(xsrc.at[0, 1], xbuf.at[2, row], xs_sem, xr_sem, across(k))
        push(ysrc.at[0], ybuf.at[2, row], ys_sem, yr_sem, along(k))
        push(ysrc.at[0], ybuf.at[2, row], ys_sem, yr_sem, across(k))

    repeat(NZ - 1, push_x0)
    push(xsrc.at[0, 1], xbuf.at[2, row], xs_sem, xr_sem, beside)
    push(ysrc.at[0], ybuf.at[2, row], ys_sem, yr_sem, beside)
    for q in range(2):
        push(ltsrc.at[q, other_half], ltex.at[q], es_sem.at[q], er_sem.at[q], beside)
        if q == 0:
            push(xsrc.at[1:3, 1], xbuf.at[0:2, 0], es_sem.at[2], er_sem.at[2], beside)
            push(ysrc.at[1:3], ybuf.at[0:2, 0], es_sem.at[3], er_sem.at[3], beside)

    def push_d(s):
        def one(k):
            push(
                d_ref.at[s, :, at_c], dv.at[s, own_half, at_c], ds_sem.at[s], dr_sem.at[s], over(k)
            )

        repeat(NC, one)

    def push_lg(q):
        await_bytes(ltex.at[q], er_sem.at[q])
        lg[q, :, at_z] = ltsrc[q, own_half, :] + ltex[q]

        def one(k):
            @pl.when(far(k) > z)
            def _():
                push(
                    lg.at[q, :, at_z], lg.at[q, :, at_z], gs_sem.at[q], gr_sem.at[q, z], along(k)
                )

        repeat(NZ - 1, one)

    def form_m(q):
        def one(k):
            @pl.when(k < z)
            def _():
                await_bytes(
                    lg.at[q, :, pl.ds(pl.multiple_of(128 * k, 128), 128)], gr_sem.at[q, k]
                )

        repeat(NZ - 1, one)
        await_bytes(dv.at[1 + q, 0:64], dr_sem.at[1 + q])
        at = pl.ds(pl.multiple_of(128 * c + 64 * x, 64), 64)
        mv[q, at, :] = dot_t(lg[q], dv[1 + q]).astype(BF16)
        repeat(
            2 * NC - 1,
            lambda k: push(mv.at[q, at], mv.at[q, at], ms_sem.at[q], mr_sem.at[q], plane(k)),
        )

    def send(p, value):
        gx[p, 0:16, at_z] = value[0:16].astype(BF16)
        gy[p, :, at_z] = value[16:17]

        def one(k):
            push(gx.at[p, 0:16, at_z], gx.at[p, 0:16, at_z], zs_sem.at[p], zr_sem.at[p], along(k))
            push(gy.at[p, :, at_z], gy.at[p, :, at_z], qs_sem.at[p], qr_sem.at[p], along(k))
            if p == W2:
                push(gx.at[p, 0:16, at_z], hx.at[2, :, at_z], hs_sem.at[2], hr_sem.at[2], across(k))

        repeat(NZ - 1, one)
        if p == W2:
            push(gx.at[p, 0:16, at_z], hx.at[2, :, at_z], hs_sem.at[2], hr_sem.at[2], beside)

    def receive(p):
        await_bytes(gx.at[p, 0:16, 0 : 128 * (NZ - 1)], zr_sem.at[p])
        await_bytes(gy.at[p, :, 0 : 128 * (NZ - 1)], qr_sem.at[p])
        gx[p, 16:32, :] = jnp.broadcast_to(gy[p], (16, 128 * NZ)).astype(BF16)

    def push_t(s):
        def one(k):
            push(t_ref.at[s], tv.at[s, :, at_c], ts_sem.at[s], tr_sem.at[s], turn(k))

        repeat(NC - 1, one)
        tv[s, :, at_c] = t_ref[s]

    def push_h(s):
        push(gx.at[WHITE[s], 0:16], hx.at[s], hs_sem.at[s], hr_sem.at[s], beside)

    def push_a(s):
        @pl.when(c == z)
        def _():
            ah[s] = gx[WHITE[s], 0:16, :]
            repeat(
                NC - 1, lambda k: push(ah.at[s], ah.at[s], as_sem.at[s], ar_sem.at[s], turn(k))
            )

    def receive_h(s):
        await_bytes(hx.at[s], hr_sem.at[s])

    def put_white(s):
        own = gx[WHITE[s], 0:16, at_z].astype(F32)
        other = hx[s, :, at_z].astype(F32)
        resp = gx[WHITE[s], 16:32, at_z].astype(F32)
        value = jnp.concatenate(
            [jnp.where(first, own, other), jnp.where(first, other, own), resp], axis=0
        )
        white_out[s] = jnp.where(first, value, pltpu.roll(value, 64, 1))

    def trail_term(s):
        await_bytes(tv.at[s, :, 0 : 128 * (NC - 1)], tr_sem.at[s])
        return dot_t(jnp.concatenate([gx[WHITE[s]], hx[s]], axis=0), tv[s])

    def gram_term(s):
        @pl.when(c != z)
        def _():
            await_bytes(ah.at[s], ar_sem.at[s])

        left = ah[s]
        pair = jnp.concatenate([gx[WHITE[s], 0:16, :], hx[s]], axis=0)
        four = jnp.concatenate([pair, pair, pair, pair], axis=0)
        return dot_t(left, four), dot_t(left, gx[WHITE[s], 16:32, :])

    push_d(0)
    push_lg(0)
    push_d(1)
    await_bytes(xbuf.at[0:2, 0], er_sem.at[2])
    await_bytes(ybuf.at[0:2, 0], er_sem.at[3])
    tile1 = xsrc[1, 0].astype(F32) + xbuf[0, 0].astype(F32)
    resp1 = ysrc[1] + ybuf[0, 0]
    send(X1, jnp.concatenate([tile1, jnp.broadcast_to(resp1, (16, 128))], axis=0))
    tile2 = xsrc[2, 0].astype(F32) + xbuf[1, 0].astype(F32)
    resp2 = ysrc[2] + ybuf[1, 0]
    start2 = jnp.concatenate([tile2, jnp.broadcast_to(resp2, (16, 128))], axis=0)
    repeat(
        2 * NC - 1, lambda k: push(l_ref.at[1], lv.at[own_half, at_c], ls_sem, lr_sem, plane(k))
    )
    push_d(2)
    await_bytes(dv.at[:, 0:64, :], own_sem.at[0])

    await_bytes(xbuf.at[2, 0 : 2 * NZ - 1], xr_sem)
    await_bytes(ybuf.at[2, 0 : 2 * NZ - 1], yr_sem)
    for k in range(NZ):
        xr[0:16, 128 * k : 128 * k + 128] = xbuf[2, 2 * k] + xbuf[2, 2 * k + 1]
        xr[16:32, 128 * k : 128 * k + 128] = jnp.broadcast_to(
            ybuf[2, 2 * k] + ybuf[2, 2 * k + 1], (16, 128)
        ).astype(BF16)
    await_bytes(dv.at[0, 0:64], dr_sem.at[0])
    send(W0, rounded(dot_t(xr[...], dv[0])))
    push_lg(1)
    form_m(0)
    push_t(0)
    receive(X1)
    value1 = dot_t(gx[X1], dv[1])

    receive(W0)
    await_bytes(mv.at[0, 0 : 64 * (2 * NC - 1)], mr_sem.at[0])
    send(W1, rounded(value1 - dot_n(gx[W0], mv[0])))
    await_bytes(lv, lr_sem)
    send(R2, start2 - dot_t(gx[W0], lv[...]))
    push_h(0)
    push_a(0)
    form_m(1)
    push_t(1)
    push_t(2)
    receive_h(0)
    put_white(0)
    trail = trail_term(0)

    receive(R2)
    value2 = dot_t(gx[R2], dv[2])
    receive(W1)
    await_bytes(mv.at[1, 0 : 64 * (2 * NC - 1)], mr_sem.at[1])
    send(W2, rounded(value2 - dot_n(gx[W1], mv[1])))
    push_h(1)
    push_a(1)
    gram, right = gram_term(0)
    receive_h(1)
    put_white(1)
    trail = trail + trail_term(1)
    gram1, right1 = gram_term(1)

    receive(W2)
    push_a(2)
    receive_h(2)
    put_white(2)
    trail = trail + trail_term(2)
    trail_out[0:16] = jnp.where(first, trail[0:16], trail[32:48])
    trail_out[16:32] = jnp.where(first, trail[32:48], trail[0:16])
    trail_out[32:48] = trail[16:32]
    gram2, right2 = gram_term(2)
    scale = 1.0 / 6144
    right_out[...] = (right + right1 + right2) * scale
    gram = (gram + gram1 + gram2) * scale
    gram = jnp.where(first, gram, pltpu.roll(gram, 16, 1))
    nb[c] = jnp.where(lane // 32 == c % 4, gram, 0.0)
    repeat(NC - 1, lambda k: push(nb.at[c], nb.at[c], ns_sem, nr_sem, turn(k)))

    await_bytes(xbuf.at[2, 0 : 2 * NZ - 1], xs_sem)
    await_bytes(ybuf.at[2, 0 : 2 * NZ - 1], ys_sem)
    for q in range(2):
        await_bytes(ltex.at[q], es_sem.at[q])
        repeat(NZ - 1 - z, lambda k: await_bytes(lg.at[q, :, 0:128], gs_sem.at[q]))
        await_bytes(mv.at[q, 0 : 64 * (2 * NC - 1)], ms_sem.at[q])
    await_bytes(xbuf.at[0:2, 0], es_sem.at[2])
    await_bytes(ybuf.at[0:2, 0], es_sem.at[3])
    repeat(2 * NC - 1, lambda k: await_bytes(lv.at[0:64, 0:128], ls_sem))
    for p in range(5):
        await_bytes(gx.at[p, 0:16, 0 : 128 * (NZ - 1)], zs_sem.at[p])
        await_bytes(gy.at[p, :, 0 : 128 * (NZ - 1)], qs_sem.at[p])
    for s in range(3):
        await_bytes(dv.at[s, 0:64], ds_sem.at[s])
        await_bytes(hx.at[s], hs_sem.at[s])
        await_bytes(tv.at[s, :, 0 : 128 * (NC - 1)], ts_sem.at[s])

        @pl.when(c == z)
        def _():
            repeat(NC - 1, lambda k: await_bytes(ah.at[s], as_sem.at[s]))

    await_bytes(nb.at[0 : NC - 1], ns_sem)
    await_bytes(nb.at[0 : NC - 1], nr_sem)
    for j in range(4):
        normal_out[:, 128 * j : 128 * j + 128] = (
            nb[4 * j] + nb[4 * j + 1] + nb[4 * j + 2] + nb[4 * j + 3]
        )


def shards(
    x_window, y_window, block_order, diag_inverse, panel_window, panel_trail, x_trail, y_trail
):
    vmem = pl.BlockSpec(memory_space=pltpu.VMEM)
    hbm = pl.BlockSpec(memory_space=pl.ANY)
    dma = pltpu.SemaphoreType.DMA
    white, trail, normal, right = pl.pallas_call(
        kernel,
        name="substitution",
        out_shape=(
            jax.ShapeDtypeStruct((3, 48, 128), F32),
            jax.ShapeDtypeStruct((48, 128), F32),
            jax.ShapeDtypeStruct((16, 512), F32),
            jax.ShapeDtypeStruct((16, 16), F32),
        ),
        in_specs=[pl.BlockSpec(memory_space=pltpu.SMEM), vmem, vmem, hbm, vmem, vmem],
        out_specs=(vmem, vmem, vmem, vmem),
        scratch_shapes=[
            pltpu.VMEM((3, 2, 16, 128), BF16),
            pltpu.VMEM((3, 1, 128), F32),
            pltpu.VMEM((3, 32, 16, 128), BF16),
            pltpu.VMEM((3, 32, 1, 128), F32),
            pltpu.VMEM((32, 2048), BF16),
            pltpu.VMEM((2, 128, 128), BF16),
            pltpu.VMEM((2, 64, 128), BF16),
            pltpu.VMEM((2, 64, 2048), BF16),
            pltpu.VMEM((2, 2048, 128), BF16),
            pltpu.VMEM((5, 32, 2048), BF16),
            pltpu.VMEM((5, 1, 2048), F32),
            pltpu.VMEM((3, 16, 2048), BF16),
            pltpu.VMEM((3, 128, 2048), BF16),
            pltpu.VMEM((128, 2048), BF16),
            pltpu.VMEM((3, 128, 2048), BF16),
            pltpu.VMEM((3, 16, 2048), BF16),
            pltpu.VMEM((16, 16, 128), F32),
            pltpu.VMEM((40, 128), F32),
            dma((1,)),
            dma,
            dma,
            dma,
            dma,
            dma((4,)),
            dma((4,)),
            dma((3,)),
            dma((3,)),
            dma,
            dma,
            dma((2,)),
            dma((2, 16)),
            dma((5,)),
            dma((5,)),
            dma((2,)),
            dma((2,)),
            dma((5,)),
            dma((5,)),
            dma((3,)),
            dma((3,)),
            dma((3,)),
            dma((3,)),
            dma((3,)),
            dma((3,)),
            dma,
            dma,
        ],
        compiler_params=pltpu.CompilerParams(
            collective_id=0, has_side_effects=True, vmem_limit_bytes=58 * 1024 * 1024
        ),
    )(
        block_order,
        x_window.transpose(0, 2, 1),
        y_window,
        diag_inverse,
        panel_window,
        panel_trail.transpose(1, 0, 2),
    )
    whitened = white[:, 0:32, 0:64].transpose(0, 2, 1).astype(BF16)
    white_resp = white[:, 32, 0:64].astype(BF16)
    trail_rhs = x_trail.astype(F32) - trail[0:32].T
    trail_resp = y_trail - trail[32]
    return whitened, white_resp, trail_rhs, trail_resp, normal, right[:, 0]


def solution(mesh):
    in_specs = (
        P(None, "row", "col"),
        P(None, "row"),
        P(),
        P(None, "row", None),
        P(None, "row", "col"),
        P("row", None, "col"),
        P("row", "col"),
        P("row"),
    )
    out_specs = (
        P(None, "row", "col"),
        P(None, "row"),
        P("row", "col"),
        P("row"),
        P("row", None),
        P("row"),
    )
    return jax.shard_map(shards, mesh=mesh, in_specs=in_specs, out_specs=out_specs, check_vma=False)
```

time: 1260 us -> 115 us (0.09)
  blocking collectives: 765 us -> 0 us
  waiting for transfers between devices: 350 us -> 0 us
  Pallas kernels: 0 us -> 110 us
  starting transfers between devices: 105 us -> 0 us
  between operations: 20.4 us -> 0.68 us
    all_gather x7 -> x0, blocking collectives: 349 us -> none  [the longest x3 162 us: shards(): lax.all_gather(residual, 'row', axis=0, tiled=True)]
    unnamed x5 -> x0, blocking collectives: 235 us -> none
    unnamed x5 -> x0, waiting for transfers between devices: 187 us -> none
    psum x3 -> x0, blocking collectives: 182 us -> none  [the longest x2 121 us: shards(): pending_resp = pending_resp - lax.psum(update_resp, 'col')]
    psum x1 -> x0, waiting for transfers between devices: 149 us -> none  [shards(): lax.psum(trail_total.astype(jnp.bfloat16), 'col').astype(jnp.float32)]
    pallas_call x0 -> x1, Pallas kernels: none -> 110 us  [shards(): pl.pallas_call(kernel, name='substitution', out_shape=(jax.ShapeDtypeStru...]
    all_to_all x3 -> x0, starting transfers between devices: 104 us -> none  [shards(): lax.all_to_all(all_rows, 'col', split_axis=0, concat_axis=1, tiled=True)]
    all_to_all x3 -> x0, waiting for transfers between devices: 14.3 us -> none  [shards(): lax.all_to_all(all_rows, 'col', split_axis=0, concat_axis=1, tiled=True)]
  transfers between devices with their start and end apart: 6 -> 0, of which waited for: 5 -> 0; matrix products, arithmetic and copies ran while one was open for 1% -> 0% of each run, Pallas kernels for 0% -> 0%
where the time goes in v2:
time: 115 us
  Pallas kernels  110 us (96%)
  local copies, waits for them, and re-layouts  2.45 us (2%)
  other arithmetic  2.03 us (2%)
    pallas_call x1, Pallas kernels, shards(): pl.pallas_call(kernel, name='substitution', out_shape=(jax.ShapeDtypeStru...  110 us

profile of v2, /device:TPU:1, one launch (start us, length us, event | category | flops | bytes accessed | tf_op | source)
XLA Modules:
  0.0 114.7 jit_solution(5476209021630452582)
XLA Ops:
  0.6 109.6 %substitution.1 = (f32[3,48,128]{2,1,0:T(8,128)}, f32[48,128]{1,0:T(8,128)}, f32[16,512]{1,0:T(8,128)}, f32[16,16]{1,0:T(8,128)}) custom-call(s32[3]{0:T(128)} %order.1, bf16[3,32,64]{2,1,0:T(8,128)(2,1)} %bitcast.12, f32[3,64]{1,0:T(4,128)} %y_ref.1, bf16[3,64,2048]{2,1,0:T(8,128)(2,1)} %d_ref.1, bf16[3,64,128]{2,1,0:T(8,128)(2,1)} %l_ref.1, ...), custom_call_target="tpu_custom_call" | custom-call | tf_op jit(solution)/shard_map/substitution/pallas_call | solution.py:408
  110.2 0.0 copy-start.3
  110.2 0.0 copy-start.1
  110.2 0.9 convert.4
  111.1 0.0 copy-done.3
  111.1 0.0 copy-start.4
  111.1 0.0 copy-start.2
  111.1 0.6 slice_reduce_fusion
  111.8 0.0 copy-done.1
  111.8 0.0 copy-done.4
  111.8 0.5 bitcast_subtract_fusion.1
  112.3 0.0 copy-done.2
  112.3 0.6 bitcast_subtract_fusion
  112.9 0.0 copy-start
  112.9 0.6 slice_bitcast_fusion
  113.5 0.6 copy.16
  114.1 0.0 copy-done
  114.1 0.6 copy.18
  (1 shorter events, 0.0 us)
Async XLA Ops:
  110.2 0.9 copy-start.3
  110.2 1.6 %copy-start.1 = (f32[48,128]{1,0:T(8,128)S(1)}, f32[48,128]{1,0:T(8,128)}, u32[]{:S(2)}) copy-start(f32[48,128]{1,0:T(8,128)} %get-tuple-element.11) | copy-start | bytes 73732
  111.1 0.7 copy-start.4
  111.1 1.2 %copy-start.2 = (bf16[128,32]{0,1:T(8,128)(2,1)S(1)}, bf16[128,32]{0,1:T(8,128)(2,1)}, u32[]{:S(2)}) copy-start(bf16[128,32]{0,1:T(8,128)(2,1)} %param.14) | copy-start | bytes 24580
  112.9 1.2 %copy-start = (f32[16,512]{1,0:T(8,128)S(1)}, f32[16,512]{1,0:T(8,128)}, u32[]{:S(2)}) copy-start(f32[16,512]{1,0:T(8,128)} %get-tuple-element.24) | copy-start | bytes 98308

commit v3 on v2

--- a/solution.py
+++ b/solution.py
@@ -10,7 +10,7 @@
 BF16 = jnp.bfloat16
 NZ = 16
 NC = 16
-X1, W0, R2, W1, W2 = range(5)
+W0, R1, R2, W1, W2 = range(5)
 WHITE = (W0, W1, W2)
 
 
@@ -64,7 +64,9 @@
     dv,
     lv,
     tv,
-    ah,
+    wp,
+    gp,
+    gq,
     nb,
     tmp,
     own_sem,
@@ -90,8 +92,12 @@
     hr_sem,
     ts_sem,
     tr_sem,
+    vs_sem,
+    vr_sem,
     as_sem,
     ar_sem,
+    rs_sem,
+    rr_sem,
     ns_sem,
     nr_sem,
 ):
@@ -115,6 +121,11 @@
     def turn(k):
         return {"row": row, "col": lax.rem(c + 1 + k, NC)}
 
+    def alike(k):
+        return lax.rem(c + 2 + 2 * k, NC)
+
+    sibling = {"row": row, "col": c + 1 - 2 * (c % 2)}
+
     def over(k):
         return {"row": 2 * z + 1 - x, "col": lax.rem(c + k, NC)}
 
@@ -140,7 +151,8 @@
     repeat(2 * NC - 1, lambda k: greet(plane(k)))
 
     pltpu.make_async_copy(d_ref, dv.at[:, own_half, :], own_sem.at[0]).start()
-    pltpu.make_async_copy(l_ref.at[1], lv.at[own_half, at_c], lr_sem).start()
+    for t in range(2):
+        pltpu.make_async_copy(l_ref.at[t], lv.at[t, own_half, at_c], lr_sem.at[t]).start()
 
     lane = lax.broadcasted_iota(jnp.int32, (16, 128), 1)
     first = x == 0
@@ -162,17 +174,16 @@
     ).astype(F32).astype(BF16)
     lane_l = lax.broadcasted_iota(jnp.int32, (128, 128), 1)
     mine_l = jnp.where(first, lane_l, 127 - lane_l) < 64
-    for q in range(2):
-        block = l_ref[2 * q]
-        turned = dot_t(eye, jnp.concatenate([block, block], axis=0))
-        ltsrc[q] = jnp.where(mine_l, turned, 0.0).astype(BF16)
-
-        def clear(k):
-            @pl.when(k > z)
-            def _():
-                lg[q, :, pl.ds(pl.multiple_of(128 * k, 128), 128)] = jnp.zeros((64, 128), BF16)
-
-        repeat(NZ, clear)
+    block = l_ref[2]
+    turned = dot_t(eye, jnp.concatenate([block, block], axis=0))
+    ltsrc[...] = jnp.where(mine_l, turned, 0.0).astype(BF16)
+
+    def clear(k):
+        @pl.when(k > z)
+        def _():
+            lg[:, pl.ds(pl.multiple_of(128 * k, 128), 128)] = jnp.zeros((64, 128), BF16)
+
+    repeat(NZ, clear)
 
     xbuf[2, row] = xsrc[0, 0]
     ybuf[2, row] = ysrc[0]
@@ -188,11 +199,9 @@
     repeat(NZ - 1, push_x0)
     push(xsrc.at[0, 1], xbuf.at[2, row], xs_sem, xr_sem, beside)
     push(ysrc.at[0], ybuf.at[2, row], ys_sem, yr_sem, beside)
-    for q in range(2):
-        push(ltsrc.at[q, other_half], ltex.at[q], es_sem.at[q], er_sem.at[q], beside)
-        if q == 0:
-            push(xsrc.at[1:3, 1], xbuf.at[0:2, 0], es_sem.at[2], er_sem.at[2], beside)
-            push(ysrc.at[1:3], ybuf.at[0:2, 0], es_sem.at[3], er_sem.at[3], beside)
+    push(ltsrc.at[other_half], ltex, es_sem.at[0], er_sem.at[0], beside)
+    push(xsrc.at[1:3, 1], xbuf.at[0:2, 0], es_sem.at[2], er_sem.at[2], beside)
+    push(ysrc.at[1:3], ybuf.at[0:2, 0], es_sem.at[3], er_sem.at[3], beside)
 
     def push_d(s):
         def one(k):
@@ -202,39 +211,53 @@
 
         repeat(NC, one)
 
-    def push_lg(q):
-        await_bytes(ltex.at[q], er_sem.at[q])
-        lg[q, :, at_z] = ltsrc[q, own_half, :] + ltex[q]
+    def push_lg():
+        await_bytes(ltex, er_sem.at[0])
+        lg[:, at_z] = ltsrc[own_half, :] + ltex[...]
 
         def one(k):
             @pl.when(far(k) > z)
             def _():
-                push(
-                    lg.at[q, :, at_z], lg.at[q, :, at_z], gs_sem.at[q], gr_sem.at[q, z], along(k)
-                )
+                push(lg.at[:, at_z], lg.at[:, at_z], gs_sem, gr_sem.at[z], along(k))
 
         repeat(NZ - 1, one)
 
-    def form_m(q):
+    def push_l(t):
+        repeat(
+            2 * NC - 1,
+            lambda k: push(
+                l_ref.at[t], lv.at[t, own_half, at_c], ls_sem.at[t], lr_sem.at[t], plane(k)
+            ),
+        )
+
+    def form_m():
         def one(k):
             @pl.when(k < z)
             def _():
-                await_bytes(
-                    lg.at[q, :, pl.ds(pl.multiple_of(128 * k, 128), 128)], gr_sem.at[q, k]
-                )
+                await_bytes(lg.at[:, pl.ds(pl.multiple_of(128 * k, 128), 128)], gr_sem.at[k])
 
         repeat(NZ - 1, one)
-        await_bytes(dv.at[1 + q, 0:64], dr_sem.at[1 + q])
+        await_bytes(dv.at[2, 0:64], dr_sem.at[2])
         at = pl.ds(pl.multiple_of(128 * c + 64 * x, 64), 64)
-        mv[q, at, :] = dot_t(lg[q], dv[1 + q]).astype(BF16)
+        mv[at, :] = dot_t(lg[...], dv[2]).astype(BF16)
+        repeat(2 * NC - 1, lambda k: push(mv.at[at], mv.at[at], ms_sem, mr_sem, plane(k)))
+
+    def push_a(s):
+        p = WHITE[s]
+        pltpu.make_async_copy(gx.at[p, 0:16, at_z], wp.at[s, c, x], ar_sem.at[s]).start()
         repeat(
             2 * NC - 1,
-            lambda k: push(mv.at[q, at], mv.at[q, at], ms_sem.at[q], mr_sem.at[q], plane(k)),
+            lambda k: push(
+                gx.at[p, 0:16, at_z], wp.at[s, c, x], as_sem.at[s], ar_sem.at[s], plane(k)
+            ),
         )
 
     def send(p, value):
         gx[p, 0:16, at_z] = value[0:16].astype(BF16)
         gy[p, :, at_z] = value[16:17]
+
+        if p == W2:
+            push_a(2)
 
         def one(k):
             push(gx.at[p, 0:16, at_z], gx.at[p, 0:16, at_z], zs_sem.at[p], zr_sem.at[p], along(k))
@@ -253,21 +276,24 @@
 
     def push_t(s):
         def one(k):
-            push(t_ref.at[s], tv.at[s, :, at_c], ts_sem.at[s], tr_sem.at[s], turn(k))
-
-        repeat(NC - 1, one)
+            peer = {"row": row, "col": alike(k)}
+            push(t_ref.at[s], tv.at[s, :, at_c], ts_sem.at[s], tr_sem.at[s], peer)
+
+        repeat(NC // 2 - 1, one)
+        push(t_ref.at[s], tv.at[s, :, at_c], vs_sem.at[s], vr_sem.at[s], sibling)
         tv[s, :, at_c] = t_ref[s]
+
+    def relay_t(s):
+        await_bytes(tv.at[s, :, 0 : 128 * (NC // 2 - 1)], tr_sem.at[s])
+
+        def one(k):
+            at = pl.ds(pl.multiple_of(128 * alike(k), 128), 128)
+            push(tv.at[s, :, at], tv.at[s, :, at], vs_sem.at[s], vr_sem.at[s], sibling)
+
+        repeat(NC // 2 - 1, one)
 
     def push_h(s):
         push(gx.at[WHITE[s], 0:16], hx.at[s], hs_sem.at[s], hr_sem.at[s], beside)
-
-    def push_a(s):
-        @pl.when(c == z)
-        def _():
-            ah[s] = gx[WHITE[s], 0:16, :]
-            repeat(
-                NC - 1, lambda k: push(ah.at[s], ah.at[s], as_sem.at[s], ar_sem.at[s], turn(k))
-            )
 
     def receive_h(s):
         await_bytes(hx.at[s], hr_sem.at[s])
@@ -282,34 +308,27 @@
         white_out[s] = jnp.where(first, value, pltpu.roll(value, 64, 1))
 
     def trail_term(s):
-        await_bytes(tv.at[s, :, 0 : 128 * (NC - 1)], tr_sem.at[s])
+        await_bytes(tv.at[s, :, 0 : 128 * (NC // 2)], vr_sem.at[s])
         return dot_t(jnp.concatenate([gx[WHITE[s]], hx[s]], axis=0), tv[s])
 
     def gram_term(s):
-        @pl.when(c != z)
-        def _():
-            await_bytes(ah.at[s], ar_sem.at[s])
-
-        left = ah[s]
-        pair = jnp.concatenate([gx[WHITE[s], 0:16, :], hx[s]], axis=0)
-        four = jnp.concatenate([pair, pair, pair, pair], axis=0)
-        return dot_t(left, four), dot_t(left, gx[WHITE[s], 16:32, :])
+        await_bytes(wp.at[s], ar_sem.at[s])
+        left = wp[s, :, x].reshape(256, 128)
+        own = wp[s, c].reshape(32, 128).astype(F32)
+        resp = jnp.broadcast_to(gy[WHITE[s], :, at_z], (32, 128))
+        groups = [jnp.where(c % 4 == j, own, resp) for j in range(4)]
+        return dot_t(left, jnp.concatenate(groups, axis=0).astype(BF16))
 
     push_d(0)
-    push_lg(0)
-    push_d(1)
+    push_l(0)
+    push_lg()
     await_bytes(xbuf.at[0:2, 0], er_sem.at[2])
     await_bytes(ybuf.at[0:2, 0], er_sem.at[3])
-    tile1 = xsrc[1, 0].astype(F32) + xbuf[0, 0].astype(F32)
-    resp1 = ysrc[1] + ybuf[0, 0]
-    send(X1, jnp.concatenate([tile1, jnp.broadcast_to(resp1, (16, 128))], axis=0))
-    tile2 = xsrc[2, 0].astype(F32) + xbuf[1, 0].astype(F32)
-    resp2 = ysrc[2] + ybuf[1, 0]
-    start2 = jnp.concatenate([tile2, jnp.broadcast_to(resp2, (16, 128))], axis=0)
-    repeat(
-        2 * NC - 1, lambda k: push(l_ref.at[1], lv.at[own_half, at_c], ls_sem, lr_sem, plane(k))
-    )
-    push_d(2)
+    starts = []
+    for s in range(1, 3):
+        tile = xsrc[s, 0].astype(F32) + xbuf[s - 1, 0].astype(F32)
+        resp = jnp.broadcast_to(ysrc[s] + ybuf[s - 1, 0], (16, 128))
+        starts.append(jnp.concatenate([tile, resp], axis=0))
     await_bytes(dv.at[:, 0:64, :], own_sem.at[0])
 
     await_bytes(xbuf.at[2, 0 : 2 * NZ - 1], xr_sem)
@@ -321,75 +340,85 @@
         ).astype(BF16)
     await_bytes(dv.at[0, 0:64], dr_sem.at[0])
     send(W0, rounded(dot_t(xr[...], dv[0])))
-    push_lg(1)
-    form_m(0)
-    push_t(0)
-    receive(X1)
-    value1 = dot_t(gx[X1], dv[1])
+    push_d(1)
+    push_l(1)
+    push_d(2)
+    push_a(0)
 
     receive(W0)
-    await_bytes(mv.at[0, 0 : 64 * (2 * NC - 1)], mr_sem.at[0])
-    send(W1, rounded(value1 - dot_n(gx[W0], mv[0])))
-    await_bytes(lv, lr_sem)
-    send(R2, start2 - dot_t(gx[W0], lv[...]))
+    await_bytes(lv.at[0], lr_sem.at[0])
+    send(R1, starts[0] - dot_t(gx[W0], lv[0]))
+    form_m()
+    await_bytes(lv.at[1], lr_sem.at[1])
+    send(R2, starts[1] - dot_t(gx[W0], lv[1]))
     push_h(0)
-    push_a(0)
-    form_m(1)
-    push_t(1)
-    push_t(2)
+
+    await_bytes(dv.at[1, 0:64], dr_sem.at[1])
+    receive(R1)
+    send(W1, rounded(dot_t(gx[R1], dv[1])))
+    push_a(1)
+    for s in range(3):
+        push_t(s)
+    receive(R2)
+    value2 = dot_t(gx[R2], dv[2])
     receive_h(0)
     put_white(0)
+    gram = gram_term(0)
+
+    receive(W1)
+    await_bytes(mv.at[0 : 64 * (2 * NC - 1)], mr_sem)
+    send(W2, rounded(value2 - dot_n(gx[W1], mv[...])))
+    push_h(1)
+    gram = gram + gram_term(1)
+
+    gram = (gram + gram_term(2)) * (1.0 / 6144)
+    gp[...] = gram.reshape(16, 16, 128)
+    repeat(NZ - 1, lambda k: push(gp.at[far(k)], gq.at[z], rs_sem, rr_sem, along(k)))
+    gq[z] = gp[z]
+    for s in range(3):
+        relay_t(s)
     trail = trail_term(0)
-
-    receive(R2)
-    value2 = dot_t(gx[R2], dv[2])
-    receive(W1)
-    await_bytes(mv.at[1, 0 : 64 * (2 * NC - 1)], mr_sem.at[1])
-    send(W2, rounded(value2 - dot_n(gx[W1], mv[1])))
-    push_h(1)
-    push_a(1)
-    gram, right = gram_term(0)
     receive_h(1)
     put_white(1)
     trail = trail + trail_term(1)
-    gram1, right1 = gram_term(1)
 
     receive(W2)
-    push_a(2)
     receive_h(2)
     put_white(2)
     trail = trail + trail_term(2)
     trail_out[0:16] = jnp.where(first, trail[0:16], trail[32:48])
     trail_out[16:32] = jnp.where(first, trail[32:48], trail[0:16])
     trail_out[32:48] = trail[16:32]
-    gram2, right2 = gram_term(2)
-    scale = 1.0 / 6144
-    right_out[...] = (right + right1 + right2) * scale
-    gram = (gram + gram1 + gram2) * scale
-    gram = jnp.where(first, gram, pltpu.roll(gram, 16, 1))
+    await_bytes(gq.at[0 : NZ - 1], rr_sem)
+    gram = gq[0]
+    for k in range(1, NZ):
+        gram = gram + gq[k]
     nb[c] = jnp.where(lane // 32 == c % 4, gram, 0.0)
     repeat(NC - 1, lambda k: push(nb.at[c], nb.at[c], ns_sem, nr_sem, turn(k)))
+    spare = jnp.where(c % 4 == 0, 32, 0)
+    right = jnp.sum(jnp.where(lane == spare, gram, 0.0), axis=1, keepdims=True)
+    right_out[...] = jnp.broadcast_to(right, (16, 128))
+    await_bytes(gq.at[0 : NZ - 1], rs_sem)
 
     await_bytes(xbuf.at[2, 0 : 2 * NZ - 1], xs_sem)
     await_bytes(ybuf.at[2, 0 : 2 * NZ - 1], ys_sem)
-    for q in range(2):
-        await_bytes(ltex.at[q], es_sem.at[q])
-        repeat(NZ - 1 - z, lambda k: await_bytes(lg.at[q, :, 0:128], gs_sem.at[q]))
-        await_bytes(mv.at[q, 0 : 64 * (2 * NC - 1)], ms_sem.at[q])
+    await_bytes(ltex, es_sem.at[0])
+    repeat(NZ - 1 - z, lambda k: await_bytes(lg.at[:, 0:128], gs_sem))
+    await_bytes(mv.at[0 : 64 * (2 * NC - 1)], ms_sem)
     await_bytes(xbuf.at[0:2, 0], es_sem.at[2])
     await_bytes(ybuf.at[0:2, 0], es_sem.at[3])
-    repeat(2 * NC - 1, lambda k: await_bytes(lv.at[0:64, 0:128], ls_sem))
+    for t in range(2):
+        repeat(2 * NC - 1, lambda k: await_bytes(lv.at[t, 0:64, 0:128], ls_sem.at[t]))
     for p in range(5):
         await_bytes(gx.at[p, 0:16, 0 : 128 * (NZ - 1)], zs_sem.at[p])
         await_bytes(gy.at[p, :, 0 : 128 * (NZ - 1)], qs_sem.at[p])
     for s in range(3):
         await_bytes(dv.at[s, 0:64], ds_sem.at[s])
         await_bytes(hx.at[s], hs_sem.at[s])
-        await_bytes(tv.at[s, :, 0 : 128 * (NC - 1)], ts_sem.at[s])
-
-        @pl.when(c == z)
-        def _():
-            repeat(NC - 1, lambda k: await_bytes(ah.at[s], as_sem.at[s]))
+        await_bytes(tv.at[s, :, 0 : 128 * (NC // 2 - 1)], ts_sem.at[s])
+        await_bytes(tv.at[s, :, 0 : 128 * (NC // 2)], vs_sem.at[s])
+
+        repeat(2 * NC - 1, lambda k: await_bytes(wp.at[s, 0, 0], as_sem.at[s]))
 
     await_bytes(nb.at[0 : NC - 1], ns_sem)
     await_bytes(nb.at[0 : NC - 1], nr_sem)
@@ -412,7 +441,7 @@
             jax.ShapeDtypeStruct((3, 48, 128), F32),
             jax.ShapeDtypeStruct((48, 128), F32),
             jax.ShapeDtypeStruct((16, 512), F32),
-            jax.ShapeDtypeStruct((16, 16), F32),
+            jax.ShapeDtypeStruct((16, 128), F32),
         ),
         in_specs=[pl.BlockSpec(memory_space=pltpu.SMEM), vmem, vmem, hbm, vmem, vmem],
         out_specs=(vmem, vmem, vmem, vmem),
@@ -422,17 +451,19 @@
             pltpu.VMEM((3, 32, 16, 128), BF16),
             pltpu.VMEM((3, 32, 1, 128), F32),
             pltpu.VMEM((32, 2048), BF16),
-            pltpu.VMEM((2, 128, 128), BF16),
-            pltpu.VMEM((2, 64, 128), BF16),
-            pltpu.VMEM((2, 64, 2048), BF16),
-            pltpu.VMEM((2, 2048, 128), BF16),
+            pltpu.VMEM((128, 128), BF16),
+            pltpu.VMEM((64, 128), BF16),
+            pltpu.VMEM((64, 2048), BF16),
+            pltpu.VMEM((2048, 128), BF16),
             pltpu.VMEM((5, 32, 2048), BF16),
             pltpu.VMEM((5, 1, 2048), F32),
             pltpu.VMEM((3, 16, 2048), BF16),
             pltpu.VMEM((3, 128, 2048), BF16),
-            pltpu.VMEM((128, 2048), BF16),
+            pltpu.VMEM((2, 128, 2048), BF16),
             pltpu.VMEM((3, 128, 2048), BF16),
-            pltpu.VMEM((3, 16, 2048), BF16),
+            pltpu.VMEM((3, 16, 2, 16, 128), BF16),
+            pltpu.VMEM((16, 16, 128), F32),
+            pltpu.VMEM((16, 16, 128), F32),
             pltpu.VMEM((16, 16, 128), F32),
             pltpu.VMEM((40, 128), F32),
             dma((1,)),
@@ -444,14 +475,14 @@
             dma((4,)),
             dma((3,)),
             dma((3,)),
-            dma,
-            dma,
             dma((2,)),
-            dma((2, 16)),
+            dma((2,)),
+            dma,
+            dma((16,)),
             dma((5,)),
             dma((5,)),
-            dma((2,)),
-            dma((2,)),
+            dma,
+            dma,
             dma((5,)),
             dma((5,)),
             dma((3,)),
@@ -460,6 +491,10 @@
             dma((3,)),
             dma((3,)),
             dma((3,)),
+            dma((3,)),
+            dma((3,)),
+            dma,
+            dma,
             dma,
             dma,
         ],

time: 115 us -> 89.9 us (0.78)
  Pallas kernels: 110 us -> 84.5 us
    pallas_call x1, Pallas kernels: 110 us -> 84.5 us  [shards(): pl.pallas_call(kernel, name='substitution', out_shape=(jax.ShapeDtypeStru...]
where the time goes in v3:
time: 89.9 us; the launch traced here: 89.6 us
  Pallas kernels  84.5 us (94%)
  local copies, waits for them, and re-layouts  2.45 us (3%)
  other arithmetic  2.03 us (2%)
    pallas_call x1, Pallas kernels, shards(): pl.pallas_call(kernel, name='substitution', out_shape=(jax.ShapeDtypeStru...  84.5 us

profile of v3, /device:TPU:1, one launch (start us, length us, event | category | flops | bytes accessed | tf_op | source)
XLA Modules:
  0.0 89.6 jit_solution(7831563479705138395)
XLA Ops:
  0.6 84.5 %substitution.1 = (f32[3,48,128]{2,1,0:T(8,128)}, f32[48,128]{1,0:T(8,128)}, f32[16,512]{1,0:T(8,128)}, f32[16,128]{1,0:T(8,128)}) custom-call(s32[3]{0:T(128)} %order.1, bf16[3,32,64]{2,1,0:T(8,128)(2,1)} %bitcast.12, f32[3,64]{1,0:T(4,128)} %y_ref.1, bf16[3,64,2048]{2,1,0:T(8,128)(2,1)} %d_ref.1, bf16[3,64,128]{2,1,0:T(8,128)(2,1)} %l_ref.1, ...), custom_call_target="tpu_custom_call" | custom-call | tf_op jit(solution)/shard_map/substitution/pallas_call | solution.py:437
  85.1 0.0 copy-start.3
  85.1 0.0 copy-start.1
  85.1 0.9 %convert.4 = bf16[3,48,128]{2,1,0:T(8,128)(2,1)S(1)} convert(f32[3,48,128]{2,1,0:T(8,128)} %get-tuple-element.10) | non-fusion elementwise | flops 18432 | bytes 110592 | tf_op jit(solution)/shard_map/convert.1
  86.0 0.0 copy-done.3
  86.0 0.0 copy-start.4
  86.0 0.0 copy-start.2
  86.1 0.6 slice_reduce_fusion
  86.7 0.0 copy-done.1
  86.7 0.0 copy-done.4
  86.7 0.5 bitcast_subtract_fusion.1
  87.2 0.0 copy-done.2
  87.2 0.6 bitcast_subtract_fusion
  87.8 0.0 copy-start
  87.8 0.6 slice_bitcast_fusion
  88.4 0.6 copy.16
  89.0 0.0 copy-done
  89.0 0.6 copy.18
  (1 shorter events, 0.0 us)
Async XLA Ops:
  85.1 0.9 %copy-start.3 = (f32[16,128]{1,0:T(8,128)S(1)}, f32[16,128]{1,0:T(8,128)}, u32[]{:S(2)}) copy-start(f32[16,128]{1,0:T(8,128)} %get-tuple-element.13) | copy-start | bytes 24580
  85.1 1.6 %copy-start.1 = (f32[48,128]{1,0:T(8,128)S(1)}, f32[48,128]{1,0:T(8,128)}, u32[]{:S(2)}) copy-start(f32[48,128]{1,0:T(8,128)} %get-tuple-element.11) | copy-start | bytes 73732
  86.0 0.7 copy-start.4
  86.0 1.2 %copy-start.2 = (bf16[128,32]{0,1:T(8,128)(2,1)S(1)}, bf16[128,32]{0,1:T(8,128)(2,1)}, u32[]{:S(2)}) copy-start(bf16[128,32]{0,1:T(8,128)(2,1)} %param.14) | copy-start | bytes 24580
  87.8 1.2 %copy-start = (f32[16,512]{1,0:T(8,128)S(1)}, f32[16,512]{1,0:T(8,128)}, u32[]{:S(2)}) copy-start(f32[16,512]{1,0:T(8,128)} %get-tuple-element.24) | copy-start | bytes 98308

commit v4 on v3

--- a/solution.py
+++ b/solution.py
@@ -119,7 +119,7 @@
         return {"row": 2 * far(k) + 1 - x, "col": c}
 
     def turn(k):
-        return {"row": row, "col": lax.rem(c + 1 + k, NC)}
+        return {"row": row, "col": lax.rem(c + 1 + lax.rem(k + 8, NC - 1), NC)}
 
     def alike(k):
         return lax.rem(c + 2 + 2 * k, NC)
@@ -130,7 +130,7 @@
         return {"row": 2 * z + 1 - x, "col": lax.rem(c + k, NC)}
 
     def plane(k):
-        other = lax.rem(spot + 1 + k, 2 * NC)
+        other = lax.rem(spot + 1 + lax.rem(k + 9, 2 * NC - 1), 2 * NC)
         return {"row": 2 * z + other // NC, "col": other % NC}
 
     def push(src, dst, send_sem, recv_sem, peer):
@@ -305,7 +305,7 @@
         value = jnp.concatenate(
             [jnp.where(first, own, other), jnp.where(first, other, own), resp], axis=0
         )
-        white_out[s] = jnp.where(first, value, pltpu.roll(value, 64, 1))
+        white_out[s] = jnp.where(first, value, pltpu.roll(value, 64, 1)).astype(BF16)
 
     def trail_term(s):
         await_bytes(tv.at[s, :, 0 : 128 * (NC // 2)], vr_sem.at[s])
@@ -438,7 +438,7 @@
         kernel,
         name="substitution",
         out_shape=(
-            jax.ShapeDtypeStruct((3, 48, 128), F32),
+            jax.ShapeDtypeStruct((3, 48, 128), BF16),
             jax.ShapeDtypeStruct((48, 128), F32),
             jax.ShapeDtypeStruct((16, 512), F32),
             jax.ShapeDtypeStruct((16, 128), F32),
@@ -509,8 +509,8 @@
         panel_window,
         panel_trail.transpose(1, 0, 2),
     )
-    whitened = white[:, 0:32, 0:64].transpose(0, 2, 1).astype(BF16)
-    white_resp = white[:, 32, 0:64].astype(BF16)
+    whitened = white[:, 0:32, 0:64].transpose(0, 2, 1)
+    white_resp = white[:, 32, 0:64]
     trail_rhs = x_trail.astype(F32) - trail[0:32].T
     trail_resp = y_trail - trail[32]
     return whitened, white_resp, trail_rhs, trail_resp, normal, right[:, 0]

time: 89.9 us -> 90.6 us (level)
  local copies, waits for them, and re-layouts: 2.45 us -> 3.92 us
  other arithmetic: 2.03 us -> 1.12 us
    transpose x0 -> x1, local copies, waits for them, and re-layouts: none -> 1.36 us  [shards(): whitened = white[:, 0:32, 0:64].transpose(0, 2, 1)]
where the time goes in v4:
time: 90.6 us; the launch traced here: 90.3 us
  Pallas kernels  84.6 us (93%)
  local copies, waits for them, and re-layouts  3.92 us (4%)
  other arithmetic  1.12 us (1%)
    pallas_call x1, Pallas kernels, shards(): pl.pallas_call(kernel, name='substitution', out_shape=(jax.ShapeDtypeStru...  84.6 us

profile of v4, /device:TPU:1, one launch (start us, length us, event | category | flops | bytes accessed | tf_op | source)
XLA Modules:
  0.0 90.3 jit_solution(352659675058304787)
XLA Ops:
  0.6 84.6 %substitution.1 = (bf16[3,48,128]{2,1,0:T(8,128)(2,1)}, f32[48,128]{1,0:T(8,128)}, f32[16,512]{1,0:T(8,128)}, f32[16,128]{1,0:T(8,128)}) custom-call(s32[3]{0:T(128)} %order.1, bf16[3,32,64]{2,1,0:T(8,128)(2,1)} %bitcast.12, f32[3,64]{1,0:T(4,128)} %y_ref.1, bf16[3,64,2048]{2,1,0:T(8,128)(2,1)} %d_ref.1, bf16[3,64,128]{2,1,0:T(8,128)(2,1)} %l_ref.1, ...), custom_call_target="tpu_custom_call" | custom-call | tf_op jit(solution)/shard_map/substitution/pallas_call | solution.py:437
  85.3 0.0 copy-start.1
  85.3 0.0 copy-start.2
  85.3 1.4 %slice_bitcast_fusion = bf16[3,64,32]{1,2,0:T(8,128)(2,1)} fusion(bf16[3,48,128]{2,1,0:T(8,128)(2,1)} %get-tuple-element.10), kind=kLoop, calls=%fused_computation | loop fusion | bytes 24576 | tf_op jit(solution)/shard_map/transpose | solution.py:512
  86.6 0.0 copy-start
  86.6 0.7 slice.16
  87.3 0.6 copy.16
  87.9 0.0 copy-done.1
  87.9 0.0 copy-done.2
  87.9 0.0 copy-start.4
  87.9 0.0 copy-start.3
  87.9 0.6 bitcast_subtract_fusion
  88.5 0.0 copy-done.4
  88.6 0.5 bitcast_subtract_fusion.1
  89.1 0.0 copy-done.3
  89.1 0.6 slice_reduce_fusion
  89.7 0.0 copy-done
  89.7 0.6 copy.18
Async XLA Ops:
  85.3 2.7 %copy-start.1 = (f32[48,128]{1,0:T(8,128)S(1)}, f32[48,128]{1,0:T(8,128)}, u32[]{:S(2)}) copy-start(f32[48,128]{1,0:T(8,128)} %get-tuple-element.11) | copy-start | bytes 73732
  85.3 2.6 %copy-start.2 = (bf16[128,32]{0,1:T(8,128)(2,1)S(1)}, bf16[128,32]{0,1:T(8,128)(2,1)}, u32[]{:S(2)}) copy-start(bf16[128,32]{0,1:T(8,128)(2,1)} %param.14) | copy-start | bytes 24580
  86.6 3.1 %copy-start = (f32[16,512]{1,0:T(8,128)S(1)}, f32[16,512]{1,0:T(8,128)}, u32[]{:S(2)}) copy-start(f32[16,512]{1,0:T(8,128)} %get-tuple-element.24) | copy-start | bytes 98308
  87.9 0.7 copy-start.4
  87.9 1.2 %copy-start.3 = (f32[16,128]{1,0:T(8,128)S(1)}, f32[16,128]{1,0:T(8,128)}, u32[]{:S(2)}) copy-start(f32[16,128]{1,0:T(8,128)} %get-tuple-element.13) | copy-start | bytes 24580
